TPU v7x, 32 devices: a whole 2x2x4 slice. The times are simulated.
32 devices in a mesh: ctx: 8 (over z, y), head: 4 (over x, core).
Axes of the slice: x: 2, y: 2, z: 4, core: 2. Of those that a mesh axis runs over, the one named last changes fastest.
Arguments:
- lin_q: bfloat16 [1024, 2048], P('ctx', 'head'), may hold values from -5 to 5
- lin_k: bfloat16 [1024, 2048], P('ctx', 'head'), may hold values from -5 to 5
- lin_v: bfloat16 [1024, 2048], P('ctx', 'head'), may hold values from -13 to 13
- win_q: bfloat16 [1024, 2048], P('ctx', 'head'), may hold values from -5 to 5
- win_k: bfloat16 [1024, 2048], P('ctx', 'head'), may hold values from -5 to 5
- win_v: bfloat16 [1024, 2048], P('ctx', 'head'), may hold values from -5 to 5
- grad_out: bfloat16 [1024, 2048], P('ctx', 'head'), may hold values from -5 to 5
Outputs:
- mixed: bfloat16 [1024, 2048], P('ctx', 'head')
- grad_lin_q: bfloat16 [1024, 2048], P('ctx', 'head')
- grad_lin_k: bfloat16 [1024, 2048], P('ctx', 'head')
- grad_lin_v: bfloat16 [1024, 2048], P('ctx', 'head')
- grad_win_q: bfloat16 [1024, 2048], P('ctx', 'head')
- grad_win_k: bfloat16 [1024, 2048], P('ctx', 'head')
- grad_win_v: bfloat16 [1024, 2048], P('ctx', 'head')
All inputs are finite; a program needn't handle non-finite values.
Results may differ from a plain program's by a relative error of at most 0.0084.
Values may be sent and summed in bfloat16 or wider, within the bound.
A program may use at most 64 MiB of HBM per device.

v0:
```python
from functools import partial
import math

import jax
import jax.numpy as jnp
from jax import lax
from jax.sharding import PartitionSpec as P

HD = 128
WIN = 512


PRECISE = lax.Precision.HIGHEST
NORM_EPS = 1e-05


def prefix_2(value, axis, combine, identity, reverse):
    count, mine = (lax.axis_size(axis), lax.axis_index(axis))
    everything = lax.all_gather(value, axis)
    start = jnp.broadcast_to(jnp.asarray(identity, value.dtype), value.shape)

    def lap(k, before):
        at = count - 1 - k if reverse else k
        reached = at > mine if reverse else at < mine
        new = combine(before, everything[at])
        return jnp.where(reached, new, before)

    return lax.fori_loop(0, count, lap, start)


def passed_along(block, axis, distance):
    devices = range(lax.axis_size(axis))
    route = [(i - distance, i) for i in devices if i - distance in devices]
    return lax.ppermute(block, axis, route)


def shortened(value):
    return jax.tree.map(lambda a: a.astype(jnp.bfloat16) if a.dtype == jnp.float32 else a, value)


def add_states(earlier, later):
    return earlier + later


def causal_rows(block_rows):
    positions = jnp.arange(block_rows, dtype=jnp.int32)
    return positions[:, None] >= positions[None, :]


def heads_first(array):
    return jnp.moveaxis(array, 1, 0)


def heads_second(array):
    return jnp.moveaxis(array, 0, 1)


def linear_forward(query, keys, values, before):
    causal = causal_rows(query.shape[0])
    scores = jnp.einsum("thd,shd->hts", query, keys, preferred_element_type=jnp.float32)
    scores = jnp.where(causal[None], scores, 0.0)
    inner = jnp.einsum("hts,shd->thd", scores, values.astype(jnp.float32), precision=PRECISE)
    result = inner + jnp.einsum(
        "thd,hde->the", query.astype(jnp.float32), before, precision=PRECISE
    )
    return (result, scores)


def linear_backward(query, keys, values, cotangent, scores, before, after):
    causal = causal_rows(query.shape[0])
    cotangent_f = cotangent.astype(jnp.float32)
    dprobs = jnp.einsum("the,she->hts", cotangent, values, preferred_element_type=jnp.float32)
    dprobs = jnp.where(causal[None], dprobs, 0.0)
    query_grad = jnp.einsum("hts,shd->thd", dprobs, keys.astype(jnp.float32), precision=PRECISE)
    query_grad = query_grad + jnp.einsum("the,hde->thd", cotangent_f, before, precision=PRECISE)
    key_grad = jnp.einsum("hts,thd->shd", dprobs, query.astype(jnp.float32), precision=PRECISE)
    key_grad = key_grad + jnp.einsum(
        "she,hde->shd", values.astype(jnp.float32), after, precision=PRECISE
    )
    value_grad = jnp.einsum("hts,the->she", scores, cotangent_f, precision=PRECISE)
    value_grad = value_grad + jnp.einsum(
        "shd,hde->she", keys.astype(jnp.float32), after, precision=PRECISE
    )
    return (query_grad, key_grad, value_grad)


def query_head(pieces, first_pos):
    query, keys, values, upstream = pieces
    row_count = query.shape[0]
    ext_count = keys.shape[0]
    window = ext_count - row_count
    score_scale = 1.0 / math.sqrt(query.shape[1])
    scores = jnp.einsum("td,sd->ts", query, keys, preferred_element_type=jnp.float32) * score_scale
    query_pos = first_pos + jnp.arange(row_count, dtype=jnp.int32)
    key_pos = first_pos - window + jnp.arange(ext_count, dtype=jnp.int32)
    allowed = (
        (key_pos[None, :] >= 0)
        & (key_pos[None, :] <= query_pos[:, None])
        & (key_pos[None, :] > query_pos[:, None] - window)
    )
    scores = jnp.where(allowed, scores, -jnp.inf)
    row_max = jnp.max(scores, axis=1, keepdims=True)
    log_total = row_max[:, 0] + jnp.log(jnp.sum(jnp.exp(scores - row_max), axis=1))
    probs = jnp.exp(scores - log_total[:, None])
    weights_low = probs.astype(jnp.bfloat16)
    output = jnp.einsum("ts,sd->td", weights_low, values, preferred_element_type=jnp.float32)
    dprobs = jnp.einsum("td,sd->ts", upstream, values, preferred_element_type=jnp.float32)
    row_dot = jnp.sum(probs * dprobs, axis=1)
    dscores = (probs * (dprobs - row_dot[:, None]) * score_scale).astype(jnp.bfloat16)
    query_grad = jnp.einsum("ts,sd->td", dscores, keys, preferred_element_type=jnp.float32)
    return (output, query_grad, log_total, row_dot)


def key_head(pieces, first_pos, total_rows):
    query, upstream, totals, dots, keys, values = pieces
    row_count = keys.shape[0]
    ext_count = query.shape[0]
    window = ext_count - row_count
    score_scale = 1.0 / math.sqrt(query.shape[1])
    scores = jnp.einsum("td,sd->ts", query, keys, preferred_element_type=jnp.float32) * score_scale
    query_pos = first_pos + jnp.arange(ext_count, dtype=jnp.int32)
    key_pos = first_pos + jnp.arange(row_count, dtype=jnp.int32)
    allowed = (
        (query_pos[:, None] < total_rows)
        & (key_pos[None, :] <= query_pos[:, None])
        & (key_pos[None, :] > query_pos[:, None] - window)
    )
    probs = jnp.where(allowed, jnp.exp(scores - totals[:, None]), 0.0)
    weights_low = probs.astype(jnp.bfloat16)
    dprobs = jnp.einsum("td,sd->ts", upstream, values, preferred_element_type=jnp.float32)
    dscores = (probs * (dprobs - dots[:, None]) * score_scale).astype(jnp.bfloat16)
    key_grad = jnp.einsum("ts,td->sd", dscores, query, preferred_element_type=jnp.float32)
    value_grad = jnp.einsum("ts,td->sd", weights_low, upstream, preferred_element_type=jnp.float32)
    return (key_grad, value_grad)


def shards(lin_q, lin_k, lin_v, win_q, win_k, win_v, grad_out):
    row_count = lin_q.shape[0]
    head_count = lin_q.shape[1] // HD
    shaped = (row_count, head_count, HD)
    flat = (row_count, head_count * HD)
    span = WIN // row_count
    total_rows = row_count * lax.axis_size("ctx")
    first_pos = lax.axis_index("ctx") * row_count
    lin_query = lin_q.reshape(shaped)
    lin_key = lin_k.reshape(shaped)
    lin_value = lin_v.reshape(shaped)
    zero_state = jnp.zeros((head_count, HD, HD), jnp.float32)
    key_state = jnp.einsum("shd,she->hde", lin_key, lin_value, preferred_element_type=jnp.float32)
    prefix = prefix_2(key_state, "ctx", add_states, zero_state, False)
    lin_out, lin_scores = linear_forward(lin_query, lin_key, lin_value, prefix)
    upstream = grad_out.reshape(shaped).astype(jnp.float32)
    square_sum, cross_sum = lax.psum(
        (jnp.sum(lin_out * lin_out, axis=(1, 2)), jnp.sum(upstream * lin_out, axis=(1, 2))), "head"
    )
    features = head_count * HD * lax.axis_size("head")
    inv_rms = lax.rsqrt(square_sum / features + NORM_EPS)
    lin_dout = (
        inv_rms[:, None, None] * upstream
        - lin_out * (inv_rms**3 * cross_sum / features)[:, None, None]
    ).astype(jnp.bfloat16)
    query_state = jnp.einsum(
        "thd,the->hde", lin_query, lin_dout, preferred_element_type=jnp.float32
    )
    suffix = prefix_2(query_state, "ctx", add_states, zero_state, True)
    grad_q, grad_k, grad_v = linear_backward(
        lin_query, lin_key, lin_value, lin_dout, lin_scores, prefix, suffix
    )
    win_query = win_q.reshape(shaped)
    win_key = win_k.reshape(shaped)
    win_value = win_v.reshape(shaped)
    cotangent = grad_out.reshape(shaped)
    reach_rows = span * row_count

    def relay_keys(passed, unused):
        moved = passed_along((passed[0], passed[1]), "ctx", 1)
        return (moved, moved)

    last_pair, stacked = lax.scan(relay_keys, (win_key, win_value), None, length=span)
    earlier_key = stacked[0][::-1].reshape((reach_rows, head_count, HD))
    earlier_value = stacked[1][::-1].reshape((reach_rows, head_count, HD))
    key_ext = jnp.concatenate([earlier_key, win_key], axis=0)
    value_ext = jnp.concatenate([earlier_value, win_value], axis=0)
    win_out, win_dq, log_total, row_dot = lax.map(
        partial(query_head, first_pos=first_pos),
        (
            heads_first(win_query),
            heads_first(key_ext),
            heads_first(value_ext),
            heads_first(cotangent),
        ),
    )

    def relay_rows(passed, unused):
        moved_rows = passed_along(shortened(passed[0]), "ctx", -1)
        moved_stats = passed_along(passed[1], "ctx", -1)
        return ((moved_rows, moved_stats), (moved_rows, moved_stats))

    last_state, stacked_back = lax.scan(
        relay_rows, ((win_query, cotangent), (log_total, row_dot)), None, length=span
    )
    later_query = stacked_back[0][0].reshape((reach_rows, head_count, HD))
    later_upstream = stacked_back[0][1].reshape((reach_rows, head_count, HD))
    later_total = jnp.moveaxis(stacked_back[1][0], 0, 1).reshape((head_count, reach_rows))
    later_dot = jnp.moveaxis(stacked_back[1][1], 0, 1).reshape((head_count, reach_rows))
    query_ext = jnp.concatenate([win_query, later_query], axis=0)
    upstream_ext = jnp.concatenate([cotangent, later_upstream], axis=0)
    total_ext = jnp.concatenate([log_total, later_total], axis=1)
    dot_ext = jnp.concatenate([row_dot, later_dot], axis=1)
    win_dk, win_dv = lax.map(
        partial(key_head, first_pos=first_pos, total_rows=total_rows),
        (
            heads_first(query_ext),
            heads_first(upstream_ext),
            total_ext,
            dot_ext,
            heads_first(win_key),
            heads_first(win_value),
        ),
    )
    mixed = (
        (lin_out * inv_rms[:, None, None] + heads_second(win_out))
        .astype(jnp.bfloat16)
        .reshape(flat)
    )
    return (
        mixed,
        grad_q.astype(jnp.bfloat16).reshape(flat),
        grad_k.astype(jnp.bfloat16).reshape(flat),
        grad_v.astype(jnp.bfloat16).reshape(flat),
        heads_second(win_dq).astype(jnp.bfloat16).reshape(flat),
        heads_second(win_dk).astype(jnp.bfloat16).reshape(flat),
        heads_second(win_dv).astype(jnp.bfloat16).reshape(flat),
    )


def solution(mesh):
    return jax.shard_map(
        shards,
        mesh=mesh,
        in_specs=(
            P("ctx", "head"),
            P("ctx", "head"),
            P("ctx", "head"),
            P("ctx", "head"),
            P("ctx", "head"),
            P("ctx", "head"),
            P("ctx", "head"),
        ),
        out_specs=(
            P("ctx", "head"),
            P("ctx", "head"),
            P("ctx", "head"),
            P("ctx", "head"),
            P("ctx", "head"),
            P("ctx", "head"),
            P("ctx", "head"),
        ),
        check_vma=False,
    )
```

profile of v0, /device:TPU:0, one launch (start us, length us, event | category | flops | bytes accessed | tf_op | source)
XLA Modules:
  0.0 230.8 jit_solution(2791793915792682489)
XLA Ops:
  8.4 1.8 fusion.76
  14.8 57.2 %while.103 = (s32[]{:T(128)}, bf16[128,4,128]{2,1,0:T(4,128)(2,1)S(1)}, bf16[128,4,128]{2,1,0:T(4,128)(2,1)S(1)}, bf16[4,128,4,128]{3,2,1,0:T(4,128)(2,1)S(1)}, bf16[4,128,4,128]{3,2,1,0:T(4,128)(2,1)S(1)}, /*index=5*/s32[]{:T(128)}) while((s32[]{:T(128)}, bf16[128,4,128]{2,1,0:T(4,128)(2,1)S(1)}, bf16[128,4,128]{2,1,0:T(4,128)(2,1)S(1)}, ...), condition=%wide.region_5.6_spmd, body=%wide.region_4.5_spmd.sunk | while | flops 2 | bytes 2097317 | solution.py:179
  14.9 4.9 %collective-permute-start = (bf16[128,4,128]{2,1,0:T(4,128)(2,1)S(1)}, bf16[128,4,128]{2,1,0:T(4,128)(2,1)S(1)}, u32[]{:S(2)}, u32[]{:S(2)}) collective-permute-start(bf16[128,4,128]{2,1,0:T(4,128)(2,1)S(1)} %get-tuple-element.1146), channel_id=1, source_target_pairs={{0,4},{4,8},{8,12},{12,16},{16,20},{20,24},{24,28},{1,5},{5,9},{9,... | collective-permute-start | bytes 393224 | tf_op jit(solution)/shard_map/while/body/eval_jaxpr/ppermute | solution.py:34
  19.7 3.4 %collective-permute-start.1 = (bf16[128,4,128]{2,1,0:T(4,128)(2,1)S(1)}, bf16[128,4,128]{2,1,0:T(4,128)(2,1)S(1)}, u32[]{:S(2)}, u32[]{:S(2)}) collective-permute-start(bf16[128,4,128]{2,1,0:T(4,128)(2,1)S(1)} %get-tuple-element.1147), channel_id=1, source_target_pairs={{0,4},{4,8},{8,12},{12,16},{16,20},{20,24},{24,28},{1,5},{5,9},{9,... | collective-permute-start | bytes 393224 | tf_op jit(solution)/shard_map/while/body/eval_jaxpr/ppermute | solution.py:34
  23.2 1.7 collective-permute-done
  25.0 3.0 %collective-permute-done.1 = bf16[128,4,128]{2,1,0:T(4,128)(2,1)S(1)} collective-permute-done((bf16[128,4,128]{2,1,0:T(4,128)(2,1)S(1)}, bf16[128,4,128]{2,1,0:T(4,128)(2,1)S(1)}, u32[]{:S(2)}, u32[]{:S(2)}) %collective-permute-start.1) | collective-permute-done | bytes 131104 | tf_op jit(solution)/shard_map/while/body/eval_jaxpr/ppermute | solution.py:34
  28.2 4.7 %collective-permute-start = (bf16[128,4,128]{2,1,0:T(4,128)(2,1)S(1)}, bf16[128,4,128]{2,1,0:T(4,128)(2,1)S(1)}, u32[]{:S(2)}, u32[]{:S(2)}) collective-permute-start(bf16[128,4,128]{2,1,0:T(4,128)(2,1)S(1)} %get-tuple-element.1146), channel_id=1, source_target_pairs={{0,4},{4,8},{8,12},{12,16},{16,20},{20,24},{24,28},{1,5},{5,9},{9,... | collective-permute-start | bytes 393224 | tf_op jit(solution)/shard_map/while/body/eval_jaxpr/ppermute | solution.py:34
  32.9 5.3 %collective-permute-start.1 = (bf16[128,4,128]{2,1,0:T(4,128)(2,1)S(1)}, bf16[128,4,128]{2,1,0:T(4,128)(2,1)S(1)}, u32[]{:S(2)}, u32[]{:S(2)}) collective-permute-start(bf16[128,4,128]{2,1,0:T(4,128)(2,1)S(1)} %get-tuple-element.1147), channel_id=1, source_target_pairs={{0,4},{4,8},{8,12},{12,16},{16,20},{20,24},{24,28},{1,5},{5,9},{9,... | collective-permute-start | bytes 393224 | tf_op jit(solution)/shard_map/while/body/eval_jaxpr/ppermute | solution.py:34
  38.3 2.4 %collective-permute-done.1 = bf16[128,4,128]{2,1,0:T(4,128)(2,1)S(1)} collective-permute-done((bf16[128,4,128]{2,1,0:T(4,128)(2,1)S(1)}, bf16[128,4,128]{2,1,0:T(4,128)(2,1)S(1)}, u32[]{:S(2)}, u32[]{:S(2)}) %collective-permute-start.1) | collective-permute-done | bytes 131104 | tf_op jit(solution)/shard_map/while/body/eval_jaxpr/ppermute | solution.py:34
  40.8 4.4 %collective-permute-start = (bf16[128,4,128]{2,1,0:T(4,128)(2,1)S(1)}, bf16[128,4,128]{2,1,0:T(4,128)(2,1)S(1)}, u32[]{:S(2)}, u32[]{:S(2)}) collective-permute-start(bf16[128,4,128]{2,1,0:T(4,128)(2,1)S(1)} %get-tuple-element.1146), channel_id=1, source_target_pairs={{0,4},{4,8},{8,12},{12,16},{16,20},{20,24},{24,28},{1,5},{5,9},{9,... | collective-permute-start | bytes 393224 | tf_op jit(solution)/shard_map/while/body/eval_jaxpr/ppermute | solution.py:34
  45.2 9.4 %collective-permute-start.1 = (bf16[128,4,128]{2,1,0:T(4,128)(2,1)S(1)}, bf16[128,4,128]{2,1,0:T(4,128)(2,1)S(1)}, u32[]{:S(2)}, u32[]{:S(2)}) collective-permute-start(bf16[128,4,128]{2,1,0:T(4,128)(2,1)S(1)} %get-tuple-element.1147), channel_id=1, source_target_pairs={{0,4},{4,8},{8,12},{12,16},{16,20},{20,24},{24,28},{1,5},{5,9},{9,... | collective-permute-start | bytes 393224 | tf_op jit(solution)/shard_map/while/body/eval_jaxpr/ppermute | solution.py:34
  54.7 5.1 %collective-permute-done.1 = bf16[128,4,128]{2,1,0:T(4,128)(2,1)S(1)} collective-permute-done((bf16[128,4,128]{2,1,0:T(4,128)(2,1)S(1)}, bf16[128,4,128]{2,1,0:T(4,128)(2,1)S(1)}, u32[]{:S(2)}, u32[]{:S(2)}) %collective-permute-start.1) | collective-permute-done | bytes 131104 | tf_op jit(solution)/shard_map/while/body/eval_jaxpr/ppermute | solution.py:34
  60.0 4.4 %collective-permute-start = (bf16[128,4,128]{2,1,0:T(4,128)(2,1)S(1)}, bf16[128,4,128]{2,1,0:T(4,128)(2,1)S(1)}, u32[]{:S(2)}, u32[]{:S(2)}) collective-permute-start(bf16[128,4,128]{2,1,0:T(4,128)(2,1)S(1)} %get-tuple-element.1146), channel_id=1, source_target_pairs={{0,4},{4,8},{8,12},{12,16},{16,20},{20,24},{24,28},{1,5},{5,9},{9,... | collective-permute-start | bytes 393224 | tf_op jit(solution)/shard_map/while/body/eval_jaxpr/ppermute | solution.py:34
  64.4 5.0 %collective-permute-start.1 = (bf16[128,4,128]{2,1,0:T(4,128)(2,1)S(1)}, bf16[128,4,128]{2,1,0:T(4,128)(2,1)S(1)}, u32[]{:S(2)}, u32[]{:S(2)}) collective-permute-start(bf16[128,4,128]{2,1,0:T(4,128)(2,1)S(1)} %get-tuple-element.1147), channel_id=1, source_target_pairs={{0,4},{4,8},{8,12},{12,16},{16,20},{20,24},{24,28},{1,5},{5,9},{9,... | collective-permute-start | bytes 393224 | tf_op jit(solution)/shard_map/while/body/eval_jaxpr/ppermute | solution.py:34
  69.6 2.4 %collective-permute-done.1 = bf16[128,4,128]{2,1,0:T(4,128)(2,1)S(1)} collective-permute-done((bf16[128,4,128]{2,1,0:T(4,128)(2,1)S(1)}, bf16[128,4,128]{2,1,0:T(4,128)(2,1)S(1)}, u32[]{:S(2)}, u32[]{:S(2)}) %collective-permute-start.1) | collective-permute-done | bytes 131104 | tf_op jit(solution)/shard_map/while/body/eval_jaxpr/ppermute | solution.py:34
  73.7 8.9 %while.104 = (s32[]{:T(128)}, f32[4,128,128]{1,2,0:T(8,128)}, bf16[4,128,128]{2,1,0:T(8,128)(2,1)S(1)}, f32[4,128]{1,0:T(4,128)S(1)}, f32[4,128]{1,0:T(4,128)S(1...) while((s32[]{:T(128)}, f32[4,128,128]{1,2,0:T(8,128)}, ...), condition=%wide.region_10.11_spmd, body=%wide.region_6.10_spmd.sunk | while | flops 85444480 | bytes 3168017 | solution.py:184
  82.6 56.3 %while.105 = (s32[]{:T(128)}, bf16[128,4,128]{2,1,0:T(4,128)(2,1)}, bf16[128,4,128]{2,1,0:T(4,128)(2,1)}, f32[4,128]{1,0:T(4,128)S(1)}, f32[4,128]{1,0:T(4,128)S...) while((s32[]{:T(128)}, bf16[128,4,128]{2,1,0:T(4,128)(2,1)}, ...), condition=%wide.region_16.17_spmd, body=%wide.region_15.16_spmd.sunk | while | flops 2 | bytes 2130205 | solution.py:199
  82.7 1.3 collective-permute-start.4
  84.0 1.3 collective-permute-start.2
  85.3 1.3 collective-permute-start.3
  88.6 5.8 %collective-permute-done.5 = f32[4,128]{1,0:T(4,128)S(1)} collective-permute-done((f32[4,128]{1,0:T(4,128)S(1)}, f32[4,128]{1,0:T(4,128)S(1)}, u32[]{:S(2)}, u32[]{:S(2)}) %collective-permute-start.5) | collective-permute-done | bytes 2080 | tf_op jit(solution)/shard_map/while/body/eval_jaxpr/ppermute | solution.py:34
  102.8 5.8 %collective-permute-done.5 = f32[4,128]{1,0:T(4,128)S(1)} collective-permute-done((f32[4,128]{1,0:T(4,128)S(1)}, f32[4,128]{1,0:T(4,128)S(1)}, u32[]{:S(2)}, u32[]{:S(2)}) %collective-permute-start.5) | collective-permute-done | bytes 2080 | tf_op jit(solution)/shard_map/while/body/eval_jaxpr/ppermute | solution.py:34
  117.0 5.8 %collective-permute-done.5 = f32[4,128]{1,0:T(4,128)S(1)} collective-permute-done((f32[4,128]{1,0:T(4,128)S(1)}, f32[4,128]{1,0:T(4,128)S(1)}, u32[]{:S(2)}, u32[]{:S(2)}) %collective-permute-start.5) | collective-permute-done | bytes 2080 | tf_op jit(solution)/shard_map/while/body/eval_jaxpr/ppermute | solution.py:34
  126.1 1.3 collective-permute-start.2
  127.4 1.3 collective-permute-start.3
  128.7 1.3 collective-permute-start.5
  131.2 5.8 %collective-permute-done.5 = f32[4,128]{1,0:T(4,128)S(1)} collective-permute-done((f32[4,128]{1,0:T(4,128)S(1)}, f32[4,128]{1,0:T(4,128)S(1)}, u32[]{:S(2)}, u32[]{:S(2)}) %collective-permute-start.5) | collective-permute-done | bytes 2080 | tf_op jit(solution)/shard_map/while/body/eval_jaxpr/ppermute | solution.py:34
  140.9 8.5 %while.107 = (s32[]{:T(128)}, f32[4,128,128]{2,1,0:T(8,128)S(1)}, s32[]{:T(128)}, f32[8,4,128,128]{3,2,1,0:T(8,128)}, s32[]{:T(128)}, /*index=5*/s32[]{:T(128)}) while((s32[]{:T(128)}, f32[4,128,128]{2,1,0:T(8,128)S(1)}, s32[]{:T(128)}, f32[8,4,128,128]{3,2,1,0:T(8,128)}, s32[]{:T(128)}, /*index=5*/s32[]{:T(128)}) %tuple.204), condition=%wide.region_1.2_spmd.clone, body=%wide.region_0.1_spmd.clone.sunk | while | flops 196612 | bytes 786525 | solution.py:28
  149.9 5.7 %all-reduce = (f32[128]{0:T(128)S(1)}, f32[128]{0:T(128)S(1)}) all-reduce(f32[128]{0:T(128)S(1)} %get-tuple-element.731, f32[128]{0:T(128)S(1)} %get-tuple-element.730), channel_id=1, replica_groups=mesh['ctx'=8,'head'=4] {'head'}, use_global_device_ids=true, to_apply=%region_3.4 | all-reduce | flops 256 | bytes 2048 | tf_op jit(solution)/shard_map/psum | solution.py:153
  157.7 7.9 %while.106 = (s32[]{:T(128)}, bf16[4,128,128]{2,1,0:T(8,128)(2,1)S(1)}, bf16[4,128,128]{2,1,0:T(8,128)(2,1)S(1)}, s32[]{:T(128)}, bf16[4,640,128]{2,1,0:T(8,128)...) while((s32[]{:T(128)}, ...), condition=%wide.region_18.19_spmd, body=%wide.region_17.18_spmd.sunk | while | flops 84871808 | bytes 1873661 | solution.py:210
  170.7 42.4 %all-gather.7.cloned.1.call-done = f32[32,128,128]{2,1,0:T(8,128)} async-done(((f32[4,128,128]{2,1,0:T(8,128)}), f32[32,128,128]{2,1,0:T(8,128)}) %all-gather.7.cloned.1.call-update) | async-done | bytes 2097168 | tf_op jit(solution)/shard_map/all_gather | solution.py:19
  213.1 8.5 %while.108 = (s32[]{:T(128)}, f32[4,128,128]{2,1,0:T(8,128)S(1)}, s32[]{:T(128)}, f32[8,4,128,128]{3,2,1,0:T(8,128)}, s32[]{:T(128)}, /*index=5*/s32[]{:T(128)}, s32[]{:T(128)}, s32[]{:T(128)}) while((s32[]{:T(128)}, f32[4,128,128]{2,1,0:T(8,128)S(1)}, s32[]{:T(128)}, f32[8,4,128,128]{3,2,1,0:T(8,128)}, s32[]{:T(128)}, ...), condition=%wide.region_14.15_spmd.clone, body=%wide.region_13.14_spmd.clone.sunk | while | flops 196616 | bytes 786587 | solution.py:28
  (248 shorter events, 78.3 us)
Async XLA Ops:
  7.2 133.1 %copy-start = (bf16[128,512]{1,0:T(8,128)(2,1)S(1)}, bf16[128,512]{1,0:T(8,128)(2,1)}, u32[]{:S(2)}) copy-start(bf16[128,512]{1,0:T(8,128)(2,1)} %param.19) | copy-start | bytes 393220
  7.2 4.5 %copy-start.7 = (bf16[128,512]{1,0:T(8,128)(2,1)S(1)}, bf16[128,512]{1,0:T(8,128)(2,1)}, u32[]{:S(2)}) copy-start(bf16[128,512]{1,0:T(8,128)(2,1)} %param.24) | copy-start | bytes 393220
  7.2 5.5 %copy-start.8 = (bf16[128,512]{1,0:T(8,128)(2,1)S(1)}, bf16[128,512]{1,0:T(8,128)(2,1)}, u32[]{:S(2)}) copy-start(bf16[128,512]{1,0:T(8,128)(2,1)} %param.25) | copy-start | bytes 393220
  7.2 133.7 %all-gather.5.cloned.1.call-start = ((), (), s32[]{:S(2)}) async-start(), calls=%async_computation | async-start | bytes 2359296 | tf_op jit(solution)/shard_map/all_gather | solution.py:19
  8.4 4.5 %copy-start.2 = (bf16[128,512]{0,1:T(8,128)(2,1)}, bf16[128,512]{0,1:T(8,128)(2,1)S(1)}, u32[]{:S(2)}) copy-start(bf16[128,512]{0,1:T(8,128)(2,1)S(1)} %copy.207) | copy-start | bytes 393220
  10.2 202.8 %all-gather.7.cloned.1.call-start = ((), (), s32[]{:S(2)}) async-start(), calls=%async_computation.1 | async-start | bytes 2359296 | tf_op jit(solution)/shard_map/all_gather | solution.py:19
  14.9 10.1 %collective-permute-start = (bf16[128,4,128]{2,1,0:T(4,128)(2,1)S(1)}, bf16[128,4,128]{2,1,0:T(4,128)(2,1)S(1)}, u32[]{:S(2)}, u32[]{:S(2)}) collective-permute-start(bf16[128,4,128]{2,1,0:T(4,128)(2,1)S(1)} %get-tuple-element.1146), channel_id=1, source_target_pairs={{0,4},{4,8},{8,12},{12,16},{16,20},{20,24},{24,28},{1,5},{5,9},{9,... | collective-permute-start | bytes 393224 | tf_op jit(solution)/shard_map/while/body/eval_jaxpr/ppermute | solution.py:34
  19.7 8.3 %collective-permute-start.1 = (bf16[128,4,128]{2,1,0:T(4,128)(2,1)S(1)}, bf16[128,4,128]{2,1,0:T(4,128)(2,1)S(1)}, u32[]{:S(2)}, u32[]{:S(2)}) collective-permute-start(bf16[128,4,128]{2,1,0:T(4,128)(2,1)S(1)} %get-tuple-element.1147), channel_id=1, source_target_pairs={{0,4},{4,8},{8,12},{12,16},{16,20},{20,24},{24,28},{1,5},{5,9},{9,... | collective-permute-start | bytes 393224 | tf_op jit(solution)/shard_map/while/body/eval_jaxpr/ppermute | solution.py:34
  28.2 10.0 %collective-permute-start = (bf16[128,4,128]{2,1,0:T(4,128)(2,1)S(1)}, bf16[128,4,128]{2,1,0:T(4,128)(2,1)S(1)}, u32[]{:S(2)}, u32[]{:S(2)}) collective-permute-start(bf16[128,4,128]{2,1,0:T(4,128)(2,1)S(1)} %get-tuple-element.1146), channel_id=1, source_target_pairs={{0,4},{4,8},{8,12},{12,16},{16,20},{20,24},{24,28},{1,5},{5,9},{9,... | collective-permute-start | bytes 393224 | tf_op jit(solution)/shard_map/while/body/eval_jaxpr/ppermute | solution.py:34
  32.9 7.8 %collective-permute-start.1 = (bf16[128,4,128]{2,1,0:T(4,128)(2,1)S(1)}, bf16[128,4,128]{2,1,0:T(4,128)(2,1)S(1)}, u32[]{:S(2)}, u32[]{:S(2)}) collective-permute-start(bf16[128,4,128]{2,1,0:T(4,128)(2,1)S(1)} %get-tuple-element.1147), channel_id=1, source_target_pairs={{0,4},{4,8},{8,12},{12,16},{16,20},{20,24},{24,28},{1,5},{5,9},{9,... | collective-permute-start | bytes 393224 | tf_op jit(solution)/shard_map/while/body/eval_jaxpr/ppermute | solution.py:34
  40.8 13.7 %collective-permute-start = (bf16[128,4,128]{2,1,0:T(4,128)(2,1)S(1)}, bf16[128,4,128]{2,1,0:T(4,128)(2,1)S(1)}, u32[]{:S(2)}, u32[]{:S(2)}) collective-permute-start(bf16[128,4,128]{2,1,0:T(4,128)(2,1)S(1)} %get-tuple-element.1146), channel_id=1, source_target_pairs={{0,4},{4,8},{8,12},{12,16},{16,20},{20,24},{24,28},{1,5},{5,9},{9,... | collective-permute-start | bytes 393224 | tf_op jit(solution)/shard_map/while/body/eval_jaxpr/ppermute | solution.py:34
  45.2 14.6 %collective-permute-start.1 = (bf16[128,4,128]{2,1,0:T(4,128)(2,1)S(1)}, bf16[128,4,128]{2,1,0:T(4,128)(2,1)S(1)}, u32[]{:S(2)}, u32[]{:S(2)}) collective-permute-start(bf16[128,4,128]{2,1,0:T(4,128)(2,1)S(1)} %get-tuple-element.1147), channel_id=1, source_target_pairs={{0,4},{4,8},{8,12},{12,16},{16,20},{20,24},{24,28},{1,5},{5,9},{9,... | collective-permute-start | bytes 393224 | tf_op jit(solution)/shard_map/while/body/eval_jaxpr/ppermute | solution.py:34
  60.0 9.5 %collective-permute-start = (bf16[128,4,128]{2,1,0:T(4,128)(2,1)S(1)}, bf16[128,4,128]{2,1,0:T(4,128)(2,1)S(1)}, u32[]{:S(2)}, u32[]{:S(2)}) collective-permute-start(bf16[128,4,128]{2,1,0:T(4,128)(2,1)S(1)} %get-tuple-element.1146), channel_id=1, source_target_pairs={{0,4},{4,8},{8,12},{12,16},{16,20},{20,24},{24,28},{1,5},{5,9},{9,... | collective-permute-start | bytes 393224 | tf_op jit(solution)/shard_map/while/body/eval_jaxpr/ppermute | solution.py:34
  64.4 7.5 %collective-permute-start.1 = (bf16[128,4,128]{2,1,0:T(4,128)(2,1)S(1)}, bf16[128,4,128]{2,1,0:T(4,128)(2,1)S(1)}, u32[]{:S(2)}, u32[]{:S(2)}) collective-permute-start(bf16[128,4,128]{2,1,0:T(4,128)(2,1)S(1)} %get-tuple-element.1147), channel_id=1, source_target_pairs={{0,4},{4,8},{8,12},{12,16},{16,20},{20,24},{24,28},{1,5},{5,9},{9,... | collective-permute-start | bytes 393224 | tf_op jit(solution)/shard_map/while/body/eval_jaxpr/ppermute | solution.py:34
  73.7 9.0 %copy-start.6 = (bf16[4,128,4,128]{3,1,0,2:T(8,128)(2,1)S(1)}, bf16[4,128,4,128]{3,1,0,2:T(8,128)(2,1)}, u32[]{:S(2)}) copy-start(bf16[4,128,4,128]{3,1,0,2:T(8,128)(2,1)} %custom-call.7) | copy-start | bytes 1572868
  73.7 9.0 %copy-start.10 = (f32[4,4,128]{2,1,0:T(4,128)S(1)}, f32[4,4,128]{2,1,0:T(4,128)}, u32[]{:S(2)}) copy-start(f32[4,4,128]{2,1,0:T(4,128)} %custom-call.9) | copy-start | bytes 24580
  82.7 5.9 %collective-permute-start.4 = (f32[4,128]{1,0:T(4,128)S(1)}, f32[4,128]{1,0:T(4,128)S(1)}, u32[]{:S(2)}, u32[]{:S(2)}) collective-permute-start(f32[4,128]{1,0:T(4,128)S(1)} %get-tuple-element.1233), channel_id=1, source_target_pairs={{4,0},{8,4},{12,8},{16,12},{20,16},{24,20},{28,24},{5,1},{9,5},{13... | collective-permute-start | bytes 6152 | tf_op jit(solution)/shard_map/while/body/eval_jaxpr/ppermute | solution.py:34
  84.0 10.4 %collective-permute-start.2 = (bf16[128,4,128]{2,1,0:T(4,128)(2,1)}, bf16[128,4,128]{2,1,0:T(4,128)(2,1)S(1)}, u32[]{:S(2)}, u32[]{:S(2)}) collective-permute-start(bf16[128,4,128]{2,1,0:T(4,128)(2,1)} %get-tuple-element.1231), channel_id=1, source_target_pairs={{4,0},{8,4},{12,8},{16,12},{20,16},{24,20},{28,24},{5,1},{9,5},{13... | collective-permute-start | bytes 393224 | tf_op jit(solution)/shard_map/while/body/eval_jaxpr/ppermute | solution.py:34
  85.3 9.2 %collective-permute-start.3 = (bf16[128,4,128]{2,1,0:T(4,128)(2,1)}, bf16[128,4,128]{2,1,0:T(4,128)(2,1)S(1)}, u32[]{:S(2)}, u32[]{:S(2)}) collective-permute-start(bf16[128,4,128]{2,1,0:T(4,128)(2,1)} %get-tuple-element.1232), channel_id=1, source_target_pairs={{4,0},{8,4},{12,8},{16,12},{20,16},{24,20},{28,24},{5,1},{9,5},{13... | collective-permute-start | bytes 393224 | tf_op jit(solution)/shard_map/while/body/eval_jaxpr/ppermute | solution.py:34
  86.6 7.8 %collective-permute-start.5 = (f32[4,128]{1,0:T(4,128)S(1)}, f32[4,128]{1,0:T(4,128)S(1)}, u32[]{:S(2)}, u32[]{:S(2)}) collective-permute-start(f32[4,128]{1,0:T(4,128)S(1)} %get-tuple-element.1234), channel_id=1, source_target_pairs={{4,0},{8,4},{12,8},{16,12},{20,16},{24,20},{28,24},{5,1},{9,5},{13... | collective-permute-start | bytes 6152 | tf_op jit(solution)/shard_map/while/body/eval_jaxpr/ppermute | solution.py:34
  96.4 6.4 %collective-permute-start.4 = (f32[4,128]{1,0:T(4,128)S(1)}, f32[4,128]{1,0:T(4,128)S(1)}, u32[]{:S(2)}, u32[]{:S(2)}) collective-permute-start(f32[4,128]{1,0:T(4,128)S(1)} %get-tuple-element.1233), channel_id=1, source_target_pairs={{4,0},{8,4},{12,8},{16,12},{20,16},{24,20},{28,24},{5,1},{9,5},{13... | collective-permute-start | bytes 6152 | tf_op jit(solution)/shard_map/while/body/eval_jaxpr/ppermute | solution.py:34
  97.7 10.9 %collective-permute-start.2 = (bf16[128,4,128]{2,1,0:T(4,128)(2,1)}, bf16[128,4,128]{2,1,0:T(4,128)(2,1)S(1)}, u32[]{:S(2)}, u32[]{:S(2)}) collective-permute-start(bf16[128,4,128]{2,1,0:T(4,128)(2,1)} %get-tuple-element.1231), channel_id=1, source_target_pairs={{4,0},{8,4},{12,8},{16,12},{20,16},{24,20},{28,24},{5,1},{9,5},{13... | collective-permute-start | bytes 393224 | tf_op jit(solution)/shard_map/while/body/eval_jaxpr/ppermute | solution.py:34
  99.0 9.6 %collective-permute-start.3 = (bf16[128,4,128]{2,1,0:T(4,128)(2,1)}, bf16[128,4,128]{2,1,0:T(4,128)(2,1)S(1)}, u32[]{:S(2)}, u32[]{:S(2)}) collective-permute-start(bf16[128,4,128]{2,1,0:T(4,128)(2,1)} %get-tuple-element.1232), channel_id=1, source_target_pairs={{4,0},{8,4},{12,8},{16,12},{20,16},{24,20},{28,24},{5,1},{9,5},{13... | collective-permute-start | bytes 393224 | tf_op jit(solution)/shard_map/while/body/eval_jaxpr/ppermute | solution.py:34
  100.3 8.3 %collective-permute-start.5 = (f32[4,128]{1,0:T(4,128)S(1)}, f32[4,128]{1,0:T(4,128)S(1)}, u32[]{:S(2)}, u32[]{:S(2)}) collective-permute-start(f32[4,128]{1,0:T(4,128)S(1)} %get-tuple-element.1234), channel_id=1, source_target_pairs={{4,0},{8,4},{12,8},{16,12},{20,16},{24,20},{28,24},{5,1},{9,5},{13... | collective-permute-start | bytes 6152 | tf_op jit(solution)/shard_map/while/body/eval_jaxpr/ppermute | solution.py:34
  110.6 6.4 %collective-permute-start.4 = (f32[4,128]{1,0:T(4,128)S(1)}, f32[4,128]{1,0:T(4,128)S(1)}, u32[]{:S(2)}, u32[]{:S(2)}) collective-permute-start(f32[4,128]{1,0:T(4,128)S(1)} %get-tuple-element.1233), channel_id=1, source_target_pairs={{4,0},{8,4},{12,8},{16,12},{20,16},{24,20},{28,24},{5,1},{9,5},{13... | collective-permute-start | bytes 6152 | tf_op jit(solution)/shard_map/while/body/eval_jaxpr/ppermute | solution.py:34
  111.9 10.9 %collective-permute-start.2 = (bf16[128,4,128]{2,1,0:T(4,128)(2,1)}, bf16[128,4,128]{2,1,0:T(4,128)(2,1)S(1)}, u32[]{:S(2)}, u32[]{:S(2)}) collective-permute-start(bf16[128,4,128]{2,1,0:T(4,128)(2,1)} %get-tuple-element.1231), channel_id=1, source_target_pairs={{4,0},{8,4},{12,8},{16,12},{20,16},{24,20},{28,24},{5,1},{9,5},{13... | collective-permute-start | bytes 393224 | tf_op jit(solution)/shard_map/while/body/eval_jaxpr/ppermute | solution.py:34
  113.2 9.6 %collective-permute-start.3 = (bf16[128,4,128]{2,1,0:T(4,128)(2,1)}, bf16[128,4,128]{2,1,0:T(4,128)(2,1)S(1)}, u32[]{:S(2)}, u32[]{:S(2)}) collective-permute-start(bf16[128,4,128]{2,1,0:T(4,128)(2,1)} %get-tuple-element.1232), channel_id=1, source_target_pairs={{4,0},{8,4},{12,8},{16,12},{20,16},{24,20},{28,24},{5,1},{9,5},{13... | collective-permute-start | bytes 393224 | tf_op jit(solution)/shard_map/while/body/eval_jaxpr/ppermute | solution.py:34
  114.5 8.3 %collective-permute-start.5 = (f32[4,128]{1,0:T(4,128)S(1)}, f32[4,128]{1,0:T(4,128)S(1)}, u32[]{:S(2)}, u32[]{:S(2)}) collective-permute-start(f32[4,128]{1,0:T(4,128)S(1)} %get-tuple-element.1234), channel_id=1, source_target_pairs={{4,0},{8,4},{12,8},{16,12},{20,16},{24,20},{28,24},{5,1},{9,5},{13... | collective-permute-start | bytes 6152 | tf_op jit(solution)/shard_map/while/body/eval_jaxpr/ppermute | solution.py:34
  124.8 6.4 %collective-permute-start.4 = (f32[4,128]{1,0:T(4,128)S(1)}, f32[4,128]{1,0:T(4,128)S(1)}, u32[]{:S(2)}, u32[]{:S(2)}) collective-permute-start(f32[4,128]{1,0:T(4,128)S(1)} %get-tuple-element.1233), channel_id=1, source_target_pairs={{4,0},{8,4},{12,8},{16,12},{20,16},{24,20},{28,24},{5,1},{9,5},{13... | collective-permute-start | bytes 6152 | tf_op jit(solution)/shard_map/while/body/eval_jaxpr/ppermute | solution.py:34
  126.1 10.9 %collective-permute-start.2 = (bf16[128,4,128]{2,1,0:T(4,128)(2,1)}, bf16[128,4,128]{2,1,0:T(4,128)(2,1)S(1)}, u32[]{:S(2)}, u32[]{:S(2)}) collective-permute-start(bf16[128,4,128]{2,1,0:T(4,128)(2,1)} %get-tuple-element.1231), channel_id=1, source_target_pairs={{4,0},{8,4},{12,8},{16,12},{20,16},{24,20},{28,24},{5,1},{9,5},{13... | collective-permute-start | bytes 393224 | tf_op jit(solution)/shard_map/while/body/eval_jaxpr/ppermute | solution.py:34
  127.4 9.6 %collective-permute-start.3 = (bf16[128,4,128]{2,1,0:T(4,128)(2,1)}, bf16[128,4,128]{2,1,0:T(4,128)(2,1)S(1)}, u32[]{:S(2)}, u32[]{:S(2)}) collective-permute-start(bf16[128,4,128]{2,1,0:T(4,128)(2,1)} %get-tuple-element.1232), channel_id=1, source_target_pairs={{4,0},{8,4},{12,8},{16,12},{20,16},{24,20},{28,24},{5,1},{9,5},{13... | collective-permute-start | bytes 393224 | tf_op jit(solution)/shard_map/while/body/eval_jaxpr/ppermute | solution.py:34
  128.7 8.3 %collective-permute-start.5 = (f32[4,128]{1,0:T(4,128)S(1)}, f32[4,128]{1,0:T(4,128)S(1)}, u32[]{:S(2)}, u32[]{:S(2)}) collective-permute-start(f32[4,128]{1,0:T(4,128)S(1)} %get-tuple-element.1234), channel_id=1, source_target_pairs={{4,0},{8,4},{12,8},{16,12},{20,16},{24,20},{28,24},{5,1},{9,5},{13... | collective-permute-start | bytes 6152 | tf_op jit(solution)/shard_map/while/body/eval_jaxpr/ppermute | solution.py:34
  (5 other events, 11.8 us)
Sparse Core Ops, SparseCore 0:
  10.4 59.0 all-gather.4
  157.7 55.2 all-gather.6
where the time goes:
time: 232 us; the launch traced here: 231 us
  waiting for transfers between devices  84.4 us (36%)
  starting transfers between devices  62.1 us (27%)
  local copies, waits for them, and re-layouts  21.6 us (9%)
  other arithmetic  20.9 us (9%)
  matrix products  20.4 us (9%)
  between operations  14.5 us (6%)
  blocking collectives  5.67 us (2%)
    ppermute x24, starting transfers between devices, passed_along(): return lax.ppermute(block, axis, route)  62 us
    all_gather x2, waiting for transfers between devices, prefix_2(): everything = lax.all_gather(value, axis)  42.4 us
    ppermute x24, waiting for transfers between devices, passed_along(): return lax.ppermute(block, axis, route)  42 us
    select_n x16, other arithmetic, lap(): return jnp.where(reached, new, before)  16.6 us
    psum x1, blocking collectives, shards(): lax.psum((jnp.sum(lin_out * lin_out, axis=(1, 2)), jnp.sum(upstream * lin...  5.67 us
    while x24, local copies, waits for them, and re-layouts  5.63 us
    dot_general x4, matrix products, key_head(): jnp.einsum('td,sd->ts', query, keys, preferred_element_type=jnp.float32)  4.75 us
  transfers between devices with their start and end apart: 26, of which 14 were waited for; matrix products, arithmetic and copies ran while one was open for 17% of the time, Pallas kernels for 0%

commit v1 on v0

v1 whole, which is shorter than its diff:
```python
from functools import partial
import math

import jax
import jax.numpy as jnp
from jax import lax
from jax.experimental import pallas as pl
from jax.experimental.pallas import tpu as pltpu
from jax.sharding import PartitionSpec as P

HD = 128
WIN = 512
NORM_EPS = 1e-05
NEG = -1e30
MESH = pl.DeviceIdType.MESH
F32 = jnp.float32
BF16 = jnp.bfloat16

IN_NAMES = ("lq", "lk", "lv", "wq", "wk", "wv", "go")
OUT_NAMES = ("mixed", "glq", "glk", "glv", "gwq", "gwk", "gwv")


def dot_nn(a, b):
    return lax.dot_general(a, b, (((1,), (0,)), ((), ())), preferred_element_type=F32)


def dot_nt(a, b):
    return lax.dot_general(a, b, (((1,), (1,)), ((), ())), preferred_element_type=F32)


def dot_tn(a, b):
    return lax.dot_general(a, b, (((0,), (0,)), ((), ())), preferred_element_type=F32)


def repeat(low, high, step):
    if high - low <= 16:
        for k in range(low, high):
            step(k)
    else:

        def body(k, carry):
            step(k)
            return carry

        lax.fori_loop(low, high, body, 0)


def owner_count(n, state_rows):
    owners = 1
    while owners * 2 <= n and state_rows % (owners * 2 * 16) == 0:
        owners *= 2
    return owners


def kernel(n, hn, owners, span, names, *refs):
    r = dict(zip(names, refs))
    rows, cols = r["lq"].shape
    heads = cols // HD
    me = lax.axis_index("ctx")
    hme = lax.axis_index("head")
    piece = heads * HD // owners
    scale = 1.0 / math.sqrt(HD)
    features = cols * hn
    col = [slice(h * HD, (h + 1) * HD) for h in range(heads)]

    def around(k):
        return lax.rem(me + k, n)

    def remote(src, dst, send, recv, target, axis="ctx"):
        return pltpu.make_async_remote_copy(
            src_ref=src, dst_ref=dst, send_sem=send, recv_sem=recv,
            device_id={axis: target}, device_id_type=MESH,
        )

    barrier = pltpu.get_barrier_semaphore()

    def greet(k):
        pl.semaphore_signal(barrier, inc=1, device_id={"ctx": around(k)}, device_id_type=MESH)

    repeat(1, n, greet)
    for k in range(1, hn):
        pl.semaphore_signal(
            barrier, inc=1, device_id={"head": lax.rem(hme + k, hn)}, device_id_type=MESH
        )

    def rows_of(owner):
        return pl.ds(pl.multiple_of(owner * piece, piece), piece)

    def state_copy(which, k):
        target = around(k)
        return remote(
            r[which + "_own"].at[rows_of(target)], r[which + "_got"].at[me],
            r[which + "_s1"].at[target], r[which + "_r1"].at[me], target,
        )

    def total_copy(which, k):
        target = around(k)
        return remote(
            r[which + "_sums"].at[target], r[which + "_all"].at[rows_of(me)],
            r[which + "_s2"].at[target], r[which + "_r2"].at[me], target,
        )

    def when_owner(index, act):
        if owners == n:
            act()
        else:
            pl.when(index < owners)(act)

    def send_states(which):
        def one(k):
            when_owner(around(k), lambda: state_copy(which, k).start())

        repeat(1, n, one)

        def own():
            r[which + "_got"][me] = r[which + "_own"][rows_of(me), :]

        when_owner(me, own)

    def scan_states(which, reverse):
        def act():
            def arrive(k):
                source = around(k)
                remote(
                    r[which + "_own"].at[rows_of(0)], r[which + "_got"].at[source],
                    r[which + "_s1"].at[0], r[which + "_r1"].at[source], me,
                ).wait_recv()

            repeat(1, n, arrive)

            def lap(k, acc):
                at = n - 1 - k if reverse else k
                r[which + "_sums"][at] = acc.astype(BF16)
                return acc + r[which + "_got"][at].astype(F32)

            acc = jnp.zeros((piece, HD), F32)
            if n <= 16:
                for k in range(n):
                    acc = lap(k, acc)
            else:
                lax.fori_loop(0, n, lap, acc)
            repeat(1, n, lambda k: total_copy(which, k).start())
            r[which + "_all"][rows_of(me), :] = r[which + "_sums"][me]

        when_owner(me, act)

    def take_totals(which):
        def one(k):
            source = around(k)

            def act():
                remote(
                    r[which + "_sums"].at[0], r[which + "_all"].at[rows_of(source)],
                    r[which + "_s2"].at[0], r[which + "_r2"].at[source], me,
                ).wait_recv()

            when_owner(source, act)

        repeat(1, n, one)

    def finish_states(which):
        def one(k):
            when_owner(around(k), lambda: state_copy(which, k).wait_send())

        repeat(1, n, one)
        when_owner(me, lambda: repeat(1, n, lambda k: total_copy(which, k).wait_send()))

    def slot(d):
        return pl.ds(d * rows, rows)

    def halo(name, source, d):
        forward = name in ("kx", "vx")
        return remote(
            r[source], r[name].at[slot(d)],
            r[name + "_s"].at[d], r[name + "_r"].at[d], me + d if forward else me - d,
        )

    def halo_sends(d, act):
        @pl.when(me + d < n)
        def _():
            act(halo("kx", "wk", d))
            act(halo("vx", "wv", d))

        @pl.when(me - d >= 0)
        def _():
            act(halo("qx", "wq", d))
            act(halo("gx", "go", d))

    def stat_copy(d):
        return remote(
            r["stat_own"], r["stat"].at[d], r["stat_s"].at[d], r["stat_r"].at[d], me - d
        )

    def norm_copy(k):
        target = lax.rem(hme + k, hn)
        return remote(
            r["norm_own"], r["norm"].at[hme], r["norm_s"].at[target], r["norm_r"].at[hme],
            target, "head",
        )

    row_id = lax.broadcasted_iota(jnp.int32, (rows, rows), 0)
    col_id = lax.broadcasted_iota(jnp.int32, (rows, rows), 1)
    causal = row_id >= col_id
    lane = lax.broadcasted_iota(jnp.int32, (rows, HD), 1)

    for h in range(heads):
        r["ks_own"][col[h], :] = dot_tn(r["lk"][:, col[h]], r["lv"][:, col[h]]).astype(BF16)

    pl.semaphore_wait(barrier, n - 1 + hn - 1)
    send_states("ks")
    for d in range(1, span + 1):
        halo_sends(d, lambda copy: copy.start())

    zero_block = jnp.zeros((rows, cols), BF16)
    r["kx"][slot(0), :] = r["wk"][...]
    r["vx"][slot(0), :] = r["wv"][...]
    r["qx"][slot(0), :] = r["wq"][...]
    r["gx"][slot(0), :] = r["go"][...]
    for h in range(heads):
        scores = jnp.where(causal, dot_nt(r["lq"][:, col[h]], r["lk"][:, col[h]]), 0.0)
        low = scores.astype(BF16)
        r["lin_scores"][h] = low
        r["lin_out"][:, col[h]] = dot_nn(low, r["lv"][:, col[h]])

    scan_states("ks", False)

    def query_scores(d):
        at = slot(d)
        for h in range(heads):
            s = dot_nt(r["wq"][:, col[h]], r["kx"][at, col[h]]) * scale
            if d == 0:
                s = jnp.where(causal, s, NEG)
            elif d == span:
                s = jnp.where(row_id < col_id, s, NEG)
            r["s"][h, :, at] = s
            r["dp"][h, :, at] = dot_nt(r["go"][:, col[h]], r["vx"][at, col[h]])

    def query_block(d):
        @pl.when(me - d >= 0)
        def _():
            halo("kx", "wk", d).wait_recv()
            halo("vx", "wv", d).wait_recv()
            query_scores(d)

        @pl.when(me - d < 0)
        def _():
            r["kx"][slot(d), :] = zero_block
            r["vx"][slot(d), :] = zero_block
            for h in range(heads):
                r["s"][h, :, slot(d)] = jnp.full((rows, rows), NEG, F32)
                r["dp"][h, :, slot(d)] = jnp.zeros((rows, rows), F32)

    query_scores(0)

    take_totals("ks")
    square = jnp.zeros((rows, 1), F32)
    cross = jnp.zeros((rows, 1), F32)
    for h in range(heads):
        out = r["lin_out"][:, col[h]] + dot_nn(r["lq"][:, col[h]], r["ks_all"][col[h], :])
        r["lin_out"][:, col[h]] = out
        square += jnp.sum(out * out, axis=1, keepdims=True)
        cross += jnp.sum(out * r["go"][:, col[h]].astype(F32), axis=1, keepdims=True)
    norm_tile = jnp.where(lane == 0, square, jnp.where(lane == 1, cross, 0.0))
    norm_rows = norm_tile.T[:8]
    r["norm_own"][...] = norm_rows
    for k in range(1, hn):
        norm_copy(k).start()

    query_block(1)

    for k in range(1, hn):
        source = lax.rem(hme + k, hn)
        remote(
            r["norm_own"], r["norm"].at[source], r["norm_s"].at[0], r["norm_r"].at[source],
            hme, "head",
        ).wait_recv()
    r["norm"][hme] = norm_rows
    norm_sum = r["norm"][0]
    for k in range(1, hn):
        norm_sum = norm_sum + r["norm"][k]
    inv_row = lax.rsqrt(norm_sum[0:1] / features + NORM_EPS)
    pull_row = inv_row * inv_row * inv_row * norm_sum[1:2] / features
    inv = jnp.broadcast_to(inv_row, (HD, rows)).T
    pull = jnp.broadcast_to(pull_row, (HD, rows)).T
    for h in range(heads):
        out = r["lin_out"][:, col[h]]
        dout = (inv * r["go"][:, col[h]].astype(F32) - out * pull).astype(BF16)
        r["lin_dout"][:, col[h]] = dout
        r["lin_out"][:, col[h]] = out * inv
        r["qs_own"][col[h], :] = dot_tn(r["lq"][:, col[h]], dout).astype(BF16)
    send_states("qs")

    for h in range(heads):
        dout = r["lin_dout"][:, col[h]]
        back = jnp.where(causal, dot_nt(dout, r["lv"][:, col[h]]), 0.0).astype(BF16)
        grad = dot_nn(back, r["lk"][:, col[h]]) + dot_nt(dout, r["ks_all"][col[h], :])
        r["glq"][:, col[h]] = grad.astype(BF16)
        r["grad_k"][:, col[h]] = dot_tn(back, r["lq"][:, col[h]])
        r["grad_v"][:, col[h]] = dot_tn(r["lin_scores"][h], dout)

    scan_states("qs", True)

    for d in range(2, span + 1):
        query_block(d)

    stat_tile = jnp.zeros((rows, HD), F32)
    kept = []
    for h in range(heads):
        s = r["s"][h]
        top = jnp.max(s, axis=1, keepdims=True)
        e = jnp.exp(s - top)
        total = jnp.sum(e, axis=1, keepdims=True)
        probs = e * (1.0 / total)
        dp = r["dp"][h]
        dots = jnp.sum(probs * dp, axis=1, keepdims=True)
        stat_tile = jnp.where(lane == 2 * h, top + jnp.log(total), stat_tile)
        stat_tile = jnp.where(lane == 2 * h + 1, dots, stat_tile)
        r["s"][h] = probs
        kept.append(dots)
    stat_rows = stat_tile.T[: r["stat_own"].shape[0]]
    r["stat_own"][...] = stat_rows
    for d in range(1, span + 1):
        pl.when(me - d >= 0)(lambda d=d: stat_copy(d).start())
    r["stat"][0] = stat_rows
    for h in range(heads):
        probs = r["s"][h]
        ds = (probs * (r["dp"][h] - kept[h]) * scale).astype(BF16)
        mixed = r["lin_out"][:, col[h]] + dot_nn(probs.astype(BF16), r["vx"][:, col[h]])
        r["mixed"][:, col[h]] = mixed.astype(BF16)
        r["gwq"][:, col[h]] = dot_nn(ds, r["kx"][:, col[h]]).astype(BF16)

    take_totals("qs")
    for h in range(heads):
        after = r["qs_all"][col[h], :]
        grad_k = r["grad_k"][:, col[h]] + dot_nt(r["lv"][:, col[h]], after)
        grad_v = r["grad_v"][:, col[h]] + dot_nn(r["lk"][:, col[h]], after)
        r["glk"][:, col[h]] = grad_k.astype(BF16)
        r["glv"][:, col[h]] = grad_v.astype(BF16)

    for d in range(1, span + 1):

        @pl.when(me + d < n)
        def _():
            halo("qx", "wq", d).wait_recv()
            halo("gx", "go", d).wait_recv()

        @pl.when(me + d >= n)
        def _():
            r["qx"][slot(d), :] = zero_block
            r["gx"][slot(d), :] = zero_block

    for h in range(heads):
        r["s"][h] = dot_nt(r["wk"][:, col[h]], r["qx"][:, col[h]]) * scale
        r["dp"][h] = dot_nt(r["wv"][:, col[h]], r["gx"][:, col[h]])

    for d in range(1, span + 1):

        @pl.when(me + d < n)
        def _():
            stat_copy(d).wait_recv()

        @pl.when(me + d >= n)
        def _():
            r["stat"][d] = jnp.full(stat_rows.shape, -NEG, F32)

    for h in range(heads):
        for d in range(span + 1):
            at = slot(d)
            s = r["s"][h, :, at] - r["stat"][d, 2 * h : 2 * h + 1, :]
            if d == 0:
                s = jnp.where(col_id >= row_id, s, NEG)
            elif d == span:
                s = jnp.where(col_id < row_id, s, NEG)
            probs = jnp.exp(s)
            ds = probs * (r["dp"][h, :, at] - r["stat"][d, 2 * h + 1 : 2 * h + 2, :]) * scale
            r["p_low"][h, :, at] = probs.astype(BF16)
            r["ds_low"][h, :, at] = ds.astype(BF16)
        r["gwk"][:, col[h]] = dot_nn(r["ds_low"][h], r["qx"][:, col[h]]).astype(BF16)
        r["gwv"][:, col[h]] = dot_nn(r["p_low"][h], r["gx"][:, col[h]]).astype(BF16)

    finish_states("ks")
    finish_states("qs")
    for d in range(1, span + 1):
        halo_sends(d, lambda copy: copy.wait_send())
        pl.when(me - d >= 0)(lambda d=d: stat_copy(d).wait_send())
    for k in range(1, hn):
        norm_copy(k).wait_send()


def shards(n, hn, *arrays):
    rows, cols = arrays[0].shape
    heads = cols // HD
    span = WIN // rows
    owners = owner_count(n, heads * HD)
    piece = heads * HD // owners
    ext = (span + 1) * rows
    stat_rows = -(-2 * heads // 8) * 8
    dma = pltpu.SemaphoreType.DMA
    scratch = {}
    for which in ("ks", "qs"):
        scratch[which + "_own"] = pltpu.VMEM((heads * HD, HD), BF16)
        scratch[which + "_got"] = pltpu.VMEM((n, piece, HD), BF16)
        scratch[which + "_sums"] = pltpu.VMEM((n, piece, HD), BF16)
        scratch[which + "_all"] = pltpu.VMEM((heads * HD, HD), BF16)
        for sem in ("_s1", "_r1", "_s2", "_r2"):
            scratch[which + sem] = dma((n,))
    for name in ("kx", "vx", "qx", "gx"):
        scratch[name] = pltpu.VMEM((ext, cols), BF16)
        scratch[name + "_s"] = dma((span + 1,))
        scratch[name + "_r"] = dma((span + 1,))
    scratch["stat_own"] = pltpu.VMEM((stat_rows, rows), F32)
    scratch["stat"] = pltpu.VMEM((span + 1, stat_rows, rows), F32)
    scratch["stat_s"] = dma((span + 1,))
    scratch["stat_r"] = dma((span + 1,))
    scratch["norm_own"] = pltpu.VMEM((8, rows), F32)
    scratch["norm"] = pltpu.VMEM((hn, 8, rows), F32)
    scratch["norm_s"] = dma((hn,))
    scratch["norm_r"] = dma((hn,))
    scratch["lin_scores"] = pltpu.VMEM((heads, rows, rows), BF16)
    scratch["lin_out"] = pltpu.VMEM((rows, cols), F32)
    scratch["lin_dout"] = pltpu.VMEM((rows, cols), BF16)
    scratch["grad_k"] = pltpu.VMEM((rows, cols), F32)
    scratch["grad_v"] = pltpu.VMEM((rows, cols), F32)
    scratch["s"] = pltpu.VMEM((heads, rows, ext), F32)
    scratch["dp"] = pltpu.VMEM((heads, rows, ext), F32)
    scratch["p_low"] = pltpu.VMEM((heads, rows, ext), BF16)
    scratch["ds_low"] = pltpu.VMEM((heads, rows, ext), BF16)
    names = IN_NAMES + OUT_NAMES + tuple(scratch)
    flops = 2 * rows * HD * heads * (8 * ext + 14 * HD)
    vmem = pl.BlockSpec(memory_space=pltpu.VMEM)
    outs = pl.pallas_call(
        partial(kernel, n, hn, owners, span, names),
        out_shape=[jax.ShapeDtypeStruct((rows, cols), BF16)] * len(OUT_NAMES),
        in_specs=[vmem] * len(IN_NAMES),
        out_specs=[vmem] * len(OUT_NAMES),
        scratch_shapes=list(scratch.values()),
        compiler_params=pltpu.CompilerParams(
            collective_id=0, has_side_effects=True, vmem_limit_bytes=40 * 2**20
        ),
        cost_estimate=pl.CostEstimate(
            flops=flops, bytes_accessed=14 * rows * cols * 2, transcendentals=2 * heads * rows * ext
        ),
    )(*arrays)
    return tuple(outs)


def solution(mesh):
    split = P("ctx", "head")
    return jax.shard_map(
        partial(shards, mesh.shape["ctx"], mesh.shape["head"]),
        mesh=mesh,
        in_specs=(split,) * len(IN_NAMES),
        out_specs=(split,) * len(OUT_NAMES),
        check_vma=False,
    )
```

time: 232 us -> 74.2 us (0.32)
  waiting for transfers between devices: 84.4 us -> 0 us
  Pallas kernels: 0 us -> 62.4 us
  starting transfers between devices: 62.1 us -> 0 us
  other arithmetic: 20.9 us -> 0 us
  matrix products: 20.4 us -> 0 us
  between operations: 14.5 us -> 0.66 us
  local copies, waits for them, and re-layouts: 21.6 us -> 10.9 us
  blocking collectives: 5.67 us -> 0 us
    pallas_call x0 -> x1, Pallas kernels: none -> 62.4 us  [shards(): pl.pallas_call(partial(kernel, n, hn, owners, span, names), out_shape=[ja...]
    ppermute x24 -> x0, starting transfers between devices: 62 us -> none  [passed_along(): return lax.ppermute(block, axis, route)]
    all_gather x2 -> x0, waiting for transfers between devices: 42.4 us -> none  [prefix_2(): everything = lax.all_gather(value, axis)]
    ppermute x24 -> x0, waiting for transfers between devices: 42 us -> none  [passed_along(): return lax.ppermute(block, axis, route)]
    dot_general x40 -> x0, matrix products: 20.4 us -> none  [the longest x4 4.75 us: key_head(): jnp.einsum('td,sd->ts', query, keys, preferred_element_type=jnp.float32)]
    select_n x16 -> x0, other arithmetic: 16.6 us -> none  [lap(): return jnp.where(reached, new, before)]
    while x28 -> x0, local copies, waits for them, and re-layouts: 7.5 us -> none
    unnamed x32 -> x21, local copies, waits for them, and re-layouts: 4.53 us -> 10.9 us
  transfers between devices with their start and end apart: 26 -> 0, of which waited for: 14 -> 0; matrix products, arithmetic and copies ran while one was open for 17% -> 0% of each run, Pallas kernels for 0% -> 0%
where the time goes in v1:
time: 74.2 us; the launch traced here: 74 us
  Pallas kernels  62.4 us (84%)
  local copies, waits for them, and re-layouts  10.9 us (15%)
    pallas_call x1, Pallas kernels, shards(): pl.pallas_call(partial(kernel, n, hn, owners, span, names), out_shape=[ja...  62.4 us
    unnamed x21, local copies, waits for them, and re-layouts  10.9 us

profile of v1, /device:TPU:0, one launch (start us, length us, event | category | flops | bytes accessed | tf_op | source)
XLA Modules:
  0.0 74.0 jit_solution(1584162049226541549)
XLA Ops:
  0.6 0.0 copy-start
  0.6 0.9 %copy-done = bf16[128,512]{1,0:T(8,128)(2,1)S(1)} copy-done((bf16[128,512]{1,0:T(8,128)(2,1)S(1)}, bf16[128,512]{1,0:T(8,128)(2,1)}, u32[]{:S(2)}) %copy-start) | copy-done | bytes 131096
  1.5 0.0 copy-start.1
  1.5 0.9 %copy-done.1 = bf16[128,512]{1,0:T(8,128)(2,1)S(1)} copy-done((bf16[128,512]{1,0:T(8,128)(2,1)S(1)}, bf16[128,512]{1,0:T(8,128)(2,1)}, u32[]{:S(2)}) %copy-start.1) | copy-done | bytes 131096
  2.4 0.0 copy-start.2
  2.4 0.9 %copy-done.2 = bf16[128,512]{1,0:T(8,128)(2,1)S(1)} copy-done((bf16[128,512]{1,0:T(8,128)(2,1)S(1)}, bf16[128,512]{1,0:T(8,128)(2,1)}, u32[]{:S(2)}) %copy-start.2) | copy-done | bytes 131096
  3.3 0.0 copy-start.3
  3.4 0.9 %copy-done.3 = bf16[128,512]{1,0:T(8,128)(2,1)S(1)} copy-done((bf16[128,512]{1,0:T(8,128)(2,1)S(1)}, bf16[128,512]{1,0:T(8,128)(2,1)}, u32[]{:S(2)}) %copy-start.3) | copy-done | bytes 131096
  4.3 0.0 copy-start.4
  4.3 0.9 %copy-done.4 = bf16[128,512]{1,0:T(8,128)(2,1)S(1)} copy-done((bf16[128,512]{1,0:T(8,128)(2,1)S(1)}, bf16[128,512]{1,0:T(8,128)(2,1)}, u32[]{:S(2)}) %copy-start.4) | copy-done | bytes 131096
  5.2 0.0 copy-start.5
  5.2 0.9 %copy-done.5 = bf16[128,512]{1,0:T(8,128)(2,1)S(1)} copy-done((bf16[128,512]{1,0:T(8,128)(2,1)S(1)}, bf16[128,512]{1,0:T(8,128)(2,1)}, u32[]{:S(2)}) %copy-start.5) | copy-done | bytes 131096
  6.1 0.0 copy-start.6
  6.1 0.9 %copy-done.6 = bf16[128,512]{1,0:T(8,128)(2,1)S(1)} copy-done((bf16[128,512]{1,0:T(8,128)(2,1)S(1)}, bf16[128,512]{1,0:T(8,128)(2,1)}, u32[]{:S(2)}) %copy-start.6) | copy-done | bytes 131096
  7.0 62.4 %shard_map.126 = (bf16[128,512]{1,0:T(8,128)(2,1)S(1)}, bf16[128,512]{1,0:T(8,128)(2,1)S(1)}, bf16[128,512]{1,0:T(8,128)(2,1)S(1)}, bf16[128,512]{1,0:T(8,128)(2...) custom-call(bf16[128,512]{1,0:T(8,128)(2,1)S(1)} %copy-done, ...), custom_call_target="tpu_custom_call" | custom-call | flops 905969664 | bytes 1835008 | tf_op jit(solution)/shard_map/pallas_call | solution.py:431
  69.4 0.7 copy.21
  70.1 0.7 copy.22
  70.7 0.7 copy.23
  71.4 0.7 copy.24
  72.0 0.7 copy.25
  72.7 0.7 copy.26
  73.3 0.7 copy.27
Async XLA Ops:
  0.6 0.9 %copy-start = (bf16[128,512]{1,0:T(8,128)(2,1)S(1)}, bf16[128,512]{1,0:T(8,128)(2,1)}, u32[]{:S(2)}) copy-start(bf16[128,512]{1,0:T(8,128)(2,1)} %refs_0_.1) | copy-start | bytes 393220
  1.5 0.9 %copy-start.1 = (bf16[128,512]{1,0:T(8,128)(2,1)S(1)}, bf16[128,512]{1,0:T(8,128)(2,1)}, u32[]{:S(2)}) copy-start(bf16[128,512]{1,0:T(8,128)(2,1)} %refs_1_.1) | copy-start | bytes 393220
  2.4 0.9 %copy-start.2 = (bf16[128,512]{1,0:T(8,128)(2,1)S(1)}, bf16[128,512]{1,0:T(8,128)(2,1)}, u32[]{:S(2)}) copy-start(bf16[128,512]{1,0:T(8,128)(2,1)} %refs_2_.1) | copy-start | bytes 393220
  3.3 0.9 %copy-start.3 = (bf16[128,512]{1,0:T(8,128)(2,1)S(1)}, bf16[128,512]{1,0:T(8,128)(2,1)}, u32[]{:S(2)}) copy-start(bf16[128,512]{1,0:T(8,128)(2,1)} %refs_3_.1) | copy-start | bytes 393220
  4.3 0.9 %copy-start.4 = (bf16[128,512]{1,0:T(8,128)(2,1)S(1)}, bf16[128,512]{1,0:T(8,128)(2,1)}, u32[]{:S(2)}) copy-start(bf16[128,512]{1,0:T(8,128)(2,1)} %refs_4_.1) | copy-start | bytes 393220
  5.2 0.9 %copy-start.5 = (bf16[128,512]{1,0:T(8,128)(2,1)S(1)}, bf16[128,512]{1,0:T(8,128)(2,1)}, u32[]{:S(2)}) copy-start(bf16[128,512]{1,0:T(8,128)(2,1)} %refs_5_.1) | copy-start | bytes 393220
  6.1 0.9 %copy-start.6 = (bf16[128,512]{1,0:T(8,128)(2,1)S(1)}, bf16[128,512]{1,0:T(8,128)(2,1)}, u32[]{:S(2)}) copy-start(bf16[128,512]{1,0:T(8,128)(2,1)} %refs_6_.1) | copy-start | bytes 393220

commit v2 on v1

--- a/solution.py
+++ b/solution.py
@@ -17,6 +17,8 @@
 BF16 = jnp.bfloat16
 
 IN_NAMES = ("lq", "lk", "lv", "wq", "wk", "wv", "go")
+FETCH_ORDER = (1, 2, 0, 4, 3, 5, 6)
+BLOCK_OF = {"kx": "wk", "vx": "wv", "qx": "wq", "gx": "go"}
 OUT_NAMES = ("mixed", "glq", "glk", "glv", "gwq", "gwk", "gwv")
 
 
@@ -54,7 +56,7 @@
 
 def kernel(n, hn, owners, span, names, *refs):
     r = dict(zip(names, refs))
-    rows, cols = r["lq"].shape
+    rows, cols = r["lq_in"].shape
     heads = cols // HD
     me = lax.axis_index("ctx")
     hme = lax.axis_index("head")
@@ -168,23 +170,61 @@
     def slot(d):
         return pl.ds(d * rows, rows)
 
-    def halo(name, source, d):
-        forward = name in ("kx", "vx")
+    side = {"kx": 1, "vx": 1, "qx": -1, "gx": -1}
+    odd = lax.rem(me, 2) == 1
+    leads = {1: jnp.logical_not(odd), -1: odd}
+
+    def there(index):
+        return jnp.logical_and(index >= 0, index < n)
+
+    hops = {"own": (0, 2, 2), "pair": (0, 1, 1), "far": (2, 2, 4), "back": (2, -1, 1), "near": (1, 2, 3)}
+    hop_ids = {hop: i for i, hop in enumerate(hops)}
+
+    def hop_copy(name, hop):
+        sent, offset, filled = hops[hop]
+        source = r[BLOCK_OF[name] + "_in"] if sent == 0 else r[name].at[slot(sent)]
         return remote(
-            r[source], r[name].at[slot(d)],
-            r[name + "_s"].at[d], r[name + "_r"].at[d], me + d if forward else me - d,
-        )
-
-    def halo_sends(d, act):
-        @pl.when(me + d < n)
-        def _():
-            act(halo("kx", "wk", d))
-            act(halo("vx", "wv", d))
-
-        @pl.when(me - d >= 0)
-        def _():
-            act(halo("qx", "wq", d))
-            act(halo("gx", "go", d))
+            source, r[name].at[slot(filled)], r[name + "_s"].at[hop_ids[hop]],
+            r[name + "_r"].at[filled], me + side[name] * offset,
+        )
+
+    def hop_taken(name, hop):
+        sent, offset, _ = hops[hop]
+        way = side[name]
+        taken = there(me + way * offset)
+        if sent:
+            taken = jnp.logical_and(taken, there(me - way * sent))
+        if hop == "pair":
+            taken = jnp.logical_and(taken, leads[way])
+        if hop == "back":
+            taken = jnp.logical_and(taken, jnp.logical_not(leads[way]))
+        return taken
+
+    def hop_all(names, hop, act):
+        @pl.when(hop_taken(names[0], hop))
+        def _():
+            for name in names:
+                act(hop_copy(name, hop))
+
+    def arrived(names, d):
+        @pl.when(there(me - side[names[0]] * d))
+        def _():
+            for name in names:
+                remote(
+                    r[BLOCK_OF[name] + "_in"], r[name].at[slot(d)], r[name + "_s"].at[0],
+                    r[name + "_r"].at[d], me,
+                ).wait_recv()
+
+    def start(copy):
+        copy.start()
+
+    keys_side, query_side = ("kx", "vx"), ("qx", "gx")
+
+    def fetch(i):
+        name = IN_NAMES[i]
+        slot_of = {"wk": "kx", "wv": "vx", "wq": "qx", "go": "gx"}
+        target = r[slot_of[name]].at[slot(0)] if name in slot_of else r[name]
+        return pltpu.make_async_copy(r[name + "_in"], target, r["fetch"].at[i])
 
     def stat_copy(d):
         return remote(
@@ -203,19 +243,22 @@
     causal = row_id >= col_id
     lane = lax.broadcasted_iota(jnp.int32, (rows, HD), 1)
 
+    for i in FETCH_ORDER:
+        fetch(i).start()
+    fetch(1).wait()
+    fetch(2).wait()
     for h in range(heads):
         r["ks_own"][col[h], :] = dot_tn(r["lk"][:, col[h]], r["lv"][:, col[h]]).astype(BF16)
 
     pl.semaphore_wait(barrier, n - 1 + hn - 1)
     send_states("ks")
-    for d in range(1, span + 1):
-        halo_sends(d, lambda copy: copy.start())
+    for names in (keys_side, query_side):
+        hop_all(names, "own", start)
+        hop_all(names, "pair", start)
 
     zero_block = jnp.zeros((rows, cols), BF16)
-    r["kx"][slot(0), :] = r["wk"][...]
-    r["vx"][slot(0), :] = r["wv"][...]
-    r["qx"][slot(0), :] = r["wq"][...]
-    r["gx"][slot(0), :] = r["go"][...]
+    for i in FETCH_ORDER[2:]:
+        fetch(i).wait()
     for h in range(heads):
         scores = jnp.where(causal, dot_nt(r["lq"][:, col[h]], r["lk"][:, col[h]]), 0.0)
         low = scores.astype(BF16)
@@ -227,19 +270,17 @@
     def query_scores(d):
         at = slot(d)
         for h in range(heads):
-            s = dot_nt(r["wq"][:, col[h]], r["kx"][at, col[h]]) * scale
+            s = dot_nt(r["qx"][slot(0), col[h]], r["kx"][at, col[h]]) * scale
             if d == 0:
                 s = jnp.where(causal, s, NEG)
             elif d == span:
                 s = jnp.where(row_id < col_id, s, NEG)
             r["s"][h, :, at] = s
-            r["dp"][h, :, at] = dot_nt(r["go"][:, col[h]], r["vx"][at, col[h]])
+            r["dp"][h, :, at] = dot_nt(r["gx"][slot(0), col[h]], r["vx"][at, col[h]])
 
     def query_block(d):
         @pl.when(me - d >= 0)
         def _():
-            halo("kx", "wk", d).wait_recv()
-            halo("vx", "wv", d).wait_recv()
             query_scores(d)
 
         @pl.when(me - d < 0)
@@ -259,14 +300,17 @@
         out = r["lin_out"][:, col[h]] + dot_nn(r["lq"][:, col[h]], r["ks_all"][col[h], :])
         r["lin_out"][:, col[h]] = out
         square += jnp.sum(out * out, axis=1, keepdims=True)
-        cross += jnp.sum(out * r["go"][:, col[h]].astype(F32), axis=1, keepdims=True)
+        cross += jnp.sum(out * r["gx"][slot(0), col[h]].astype(F32), axis=1, keepdims=True)
     norm_tile = jnp.where(lane == 0, square, jnp.where(lane == 1, cross, 0.0))
     norm_rows = norm_tile.T[:8]
     r["norm_own"][...] = norm_rows
     for k in range(1, hn):
         norm_copy(k).start()
 
-    query_block(1)
+    for names in (keys_side, query_side):
+        arrived(names, 2)
+        hop_all(names, "far", start)
+        hop_all(names, "back", start)
 
     for k in range(1, hn):
         source = lax.rem(hme + k, hn)
@@ -284,11 +328,17 @@
     pull = jnp.broadcast_to(pull_row, (HD, rows)).T
     for h in range(heads):
         out = r["lin_out"][:, col[h]]
-        dout = (inv * r["go"][:, col[h]].astype(F32) - out * pull).astype(BF16)
+        dout = (inv * r["gx"][slot(0), col[h]].astype(F32) - out * pull).astype(BF16)
         r["lin_dout"][:, col[h]] = dout
         r["lin_out"][:, col[h]] = out * inv
         r["qs_own"][col[h], :] = dot_tn(r["lq"][:, col[h]], dout).astype(BF16)
     send_states("qs")
+
+    for names in (keys_side, query_side):
+        arrived(names, 1)
+        hop_all(names, "near", start)
+    query_block(2)
+    query_block(1)
 
     for h in range(heads):
         dout = r["lin_dout"][:, col[h]]
@@ -300,7 +350,8 @@
 
     scan_states("qs", True)
 
-    for d in range(2, span + 1):
+    for d in (3, 4):
+        arrived(keys_side, d)
         query_block(d)
 
     stat_tile = jnp.zeros((rows, HD), F32)
@@ -338,11 +389,8 @@
         r["glv"][:, col[h]] = grad_v.astype(BF16)
 
     for d in range(1, span + 1):
-
-        @pl.when(me + d < n)
-        def _():
-            halo("qx", "wq", d).wait_recv()
-            halo("gx", "go", d).wait_recv()
+        if d > 2:
+            arrived(query_side, d)
 
         @pl.when(me + d >= n)
         def _():
@@ -350,8 +398,8 @@
             r["gx"][slot(d), :] = zero_block
 
     for h in range(heads):
-        r["s"][h] = dot_nt(r["wk"][:, col[h]], r["qx"][:, col[h]]) * scale
-        r["dp"][h] = dot_nt(r["wv"][:, col[h]], r["gx"][:, col[h]])
+        r["s"][h] = dot_nt(r["kx"][slot(0), col[h]], r["qx"][:, col[h]]) * scale
+        r["dp"][h] = dot_nt(r["vx"][slot(0), col[h]], r["gx"][:, col[h]])
 
     for d in range(1, span + 1):
 
@@ -380,17 +428,32 @@
 
     finish_states("ks")
     finish_states("qs")
+    for names in (keys_side, query_side):
+        for hop in hops:
+            hop_all(names, hop, lambda copy: copy.wait_send())
     for d in range(1, span + 1):
-        halo_sends(d, lambda copy: copy.wait_send())
         pl.when(me - d >= 0)(lambda d=d: stat_copy(d).wait_send())
     for k in range(1, hn):
         norm_copy(k).wait_send()
+
+
+def write_all(*refs):
+    count = len(OUT_NAMES)
+    copies = [
+        pltpu.make_async_copy(refs[i], refs[count + i], refs[2 * count].at[i])
+        for i in range(count)
+    ]
+    for copy in copies:
+        copy.start()
+    for copy in copies:
+        copy.wait()
 
 
 def shards(n, hn, *arrays):
     rows, cols = arrays[0].shape
     heads = cols // HD
     span = WIN // rows
+    assert span == 4 and WIN % rows == 0 and n % 2 == 0
     owners = owner_count(n, heads * HD)
     piece = heads * HD // owners
     ext = (span + 1) * rows
@@ -406,8 +469,11 @@
             scratch[which + sem] = dma((n,))
     for name in ("kx", "vx", "qx", "gx"):
         scratch[name] = pltpu.VMEM((ext, cols), BF16)
-        scratch[name + "_s"] = dma((span + 1,))
+        scratch[name + "_s"] = dma((5,))
         scratch[name + "_r"] = dma((span + 1,))
+    for name in ("lq", "lk", "lv"):
+        scratch[name] = pltpu.VMEM((rows, cols), BF16)
+    scratch["fetch"] = dma((len(IN_NAMES),))
     scratch["stat_own"] = pltpu.VMEM((stat_rows, rows), F32)
     scratch["stat"] = pltpu.VMEM((span + 1, stat_rows, rows), F32)
     scratch["stat_s"] = dma((span + 1,))
@@ -425,23 +491,34 @@
     scratch["dp"] = pltpu.VMEM((heads, rows, ext), F32)
     scratch["p_low"] = pltpu.VMEM((heads, rows, ext), BF16)
     scratch["ds_low"] = pltpu.VMEM((heads, rows, ext), BF16)
-    names = IN_NAMES + OUT_NAMES + tuple(scratch)
+    names = tuple(name + "_in" for name in IN_NAMES) + OUT_NAMES + tuple(scratch)
     flops = 2 * rows * HD * heads * (8 * ext + 14 * HD)
     vmem = pl.BlockSpec(memory_space=pltpu.VMEM)
+    hbm = pl.BlockSpec(memory_space=pltpu.HBM)
     outs = pl.pallas_call(
         partial(kernel, n, hn, owners, span, names),
         out_shape=[jax.ShapeDtypeStruct((rows, cols), BF16)] * len(OUT_NAMES),
-        in_specs=[vmem] * len(IN_NAMES),
+        in_specs=[hbm] * len(IN_NAMES),
         out_specs=[vmem] * len(OUT_NAMES),
         scratch_shapes=list(scratch.values()),
         compiler_params=pltpu.CompilerParams(
-            collective_id=0, has_side_effects=True, vmem_limit_bytes=40 * 2**20
+            collective_id=0, has_side_effects=True, vmem_limit_bytes=60 * 2**20
         ),
         cost_estimate=pl.CostEstimate(
             flops=flops, bytes_accessed=14 * rows * cols * 2, transcendentals=2 * heads * rows * ext
         ),
     )(*arrays)
-    return tuple(outs)
+    shapes = [jax.ShapeDtypeStruct(out.shape, out.dtype) for out in outs]
+    return tuple(
+        pl.pallas_call(
+            write_all,
+            out_shape=shapes,
+            in_specs=[hbm] * len(OUT_NAMES),
+            out_specs=[hbm] * len(OUT_NAMES),
+            scratch_shapes=[dma((len(OUT_NAMES),))],
+            compiler_params=pltpu.CompilerParams(vmem_limit_bytes=60 * 2**20),
+        )(*outs)
+    )
 
 
 def solution(mesh):

time: 74.2 us -> 72.8 us (0.981)
  local copies, waits for them, and re-layouts: 10.9 us -> 0 us
  Pallas kernels: 62.4 us -> 72 us
    pallas_call x0 -> x1, Pallas kernels: none -> 29 us  [shards(): pl.pallas_call(write_all, out_shape=shapes, in_specs=[hbm] * len(OUT_NAME...]
    pallas_call x1, Pallas kernels: 62.4 us -> 43 us  [shards(): pl.pallas_call(partial(kernel, n, hn, owners, span, names), out_shape=[ja...]
    unnamed x21 -> x0, local copies, waits for them, and re-layouts: 10.9 us -> none
where the time goes in v2:
time: 72.8 us; the launch traced here: 72.6 us
  Pallas kernels  72 us (99%)
    pallas_call x1, Pallas kernels, shards(): pl.pallas_call(partial(kernel, n, hn, owners, span, names), out_shape=[ja...  43 us
    pallas_call x1, Pallas kernels, shards(): pl.pallas_call(write_all, out_shape=shapes, in_specs=[hbm] * len(OUT_NAME...  29 us

profile of v2, /device:TPU:0, one launch (start us, length us, event | category | flops | bytes accessed | tf_op | source)
XLA Modules:
  0.0 72.6 jit_solution(10035809945026841466)
XLA Ops:
  0.6 43.0 %shard_map.126 = (bf16[128,512]{1,0:T(8,128)(2,1)}, bf16[128,512]{1,0:T(8,128)(2,1)}, bf16[128,512]{1,0:T(8,128)(2,1)}, bf16[128,512]{1,0:T(8,128)(2,1)}, bf16[1...) custom-call(bf16[128,512]{1,0:T(8,128)(2,1)} %refs_0_.1, bf16[128,512]{1,0:T(8,128)(2,1)} %refs_1_.1, ...), custom_call_target="tpu_custom_call" | custom-call | flops 905969664 | bytes 1835008 | tf_op jit(solution)/shard_map/pallas_call | solution.py:498
  43.7 29.0 %shard_map.127 = (bf16[128,512]{1,0:T(8,128)(2,1)}, bf16[128,512]{1,0:T(8,128)(2,1)}, bf16[128,512]{1,0:T(8,128)(2,1)}, bf16[128,512]{1,0:T(8,128)(2,1)}, bf16[1...) custom-call(bf16[128,512]{1,0:T(8,128)(2,1)} %get-tuple-element.14.refs_0_, ...), custom_call_target="tpu_custom_call" | custom-call | tf_op jit(solution)/shard_map/pallas_call | solution.py:513

commit v3 on v2

--- a/solution.py
+++ b/solution.py
@@ -439,13 +439,18 @@
 
 def write_all(*refs):
     count = len(OUT_NAMES)
-    copies = [
-        pltpu.make_async_copy(refs[i], refs[count + i], refs[2 * count].at[i])
+    held, sems = refs[2 * count], refs[2 * count + 1]
+    ins = [pltpu.make_async_copy(refs[i], held.at[i], sems.at[i]) for i in range(count)]
+    outs = [
+        pltpu.make_async_copy(held.at[i], refs[count + i], sems.at[count + i])
         for i in range(count)
     ]
-    for copy in copies:
+    for copy in ins:
         copy.start()
-    for copy in copies:
+    for arrival, copy in zip(ins, outs):
+        arrival.wait()
+        copy.start()
+    for copy in outs:
         copy.wait()
 
 
@@ -515,7 +520,9 @@
             out_shape=shapes,
             in_specs=[hbm] * len(OUT_NAMES),
             out_specs=[hbm] * len(OUT_NAMES),
-            scratch_shapes=[dma((len(OUT_NAMES),))],
+            scratch_shapes=[
+                pltpu.VMEM((len(OUT_NAMES), rows, cols), BF16), dma((2 * len(OUT_NAMES),))
+            ],
             compiler_params=pltpu.CompilerParams(vmem_limit_bytes=60 * 2**20),
         )(*outs)
     )

time: 72.8 us -> 45.9 us (0.63)
  Pallas kernels: 72 us -> 45.1 us
    pallas_call x1, Pallas kernels: 29 us -> 2.03 us  [shards(): pl.pallas_call(write_all, out_shape=shapes, in_specs=[hbm] * len(OUT_NAME...]
where the time goes in v3:
time: 45.9 us; the launch traced here: 45.7 us
  Pallas kernels  45.1 us (98%)
  between operations  0.64 us (1%)
    pallas_call x1, Pallas kernels, shards(): pl.pallas_call(partial(kernel, n, hn, owners, span, names), out_shape=[ja...  43 us
    pallas_call x1, Pallas kernels, shards(): pl.pallas_call(write_all, out_shape=shapes, in_specs=[hbm] * len(OUT_NAME...  2.03 us

profile of v3, /device:TPU:0, one launch (start us, length us, event | category | flops | bytes accessed | tf_op | source)
XLA Modules:
  0.0 45.7 jit_solution(6316470814767182866)
XLA Ops:
  0.6 43.0 %shard_map.126 = (bf16[128,512]{1,0:T(8,128)(2,1)}, bf16[128,512]{1,0:T(8,128)(2,1)}, bf16[128,512]{1,0:T(8,128)(2,1)}, bf16[128,512]{1,0:T(8,128)(2,1)}, bf16[1...) custom-call(bf16[128,512]{1,0:T(8,128)(2,1)} %refs_0_.1, bf16[128,512]{1,0:T(8,128)(2,1)} %refs_1_.1, ...), custom_call_target="tpu_custom_call" | custom-call | flops 905969664 | bytes 1835008 | tf_op jit(solution)/shard_map/pallas_call | solution.py:503
  43.7 2.0 %shard_map.127 = (bf16[128,512]{1,0:T(8,128)(2,1)}, bf16[128,512]{1,0:T(8,128)(2,1)}, bf16[128,512]{1,0:T(8,128)(2,1)}, bf16[128,512]{1,0:T(8,128)(2,1)}, bf16[1...) custom-call(bf16[128,512]{1,0:T(8,128)(2,1)} %get-tuple-element.14.refs_0_, ...), custom_call_target="tpu_custom_call" | custom-call | tf_op jit(solution)/shard_map/pallas_call | solution.py:518
